TPU v7x, 512 devices: a whole 4x8x8 slice. The times are simulated.
512 devices in a mesh: dp: 32 (over y_lo, x, core), fsdp: 16 (over y_hi, z).
Axes of the slice: x: 4, y: 8 (y_hi: 2, y_lo: 4; y = y_hi * 4 + y_lo), z: 8, core: 2. Of those that a mesh axis runs over, the one named last changes fastest.
Arguments:
- partials: bfloat16 [32, 16, 2, 512, 512], P('dp', 'fsdp'), may hold values from -16 to 32, as said below
- basis_store: bfloat16 [32, 16, 2, 512, 512], P('dp', 'fsdp'), may hold values from -1 to 2
- owner_table: int32 [16], replicated, may hold values from 1 to 31, as said below
- grad: bfloat16 [16, 512, 512], P('fsdp', 'dp'), may hold values from -6 to 6
- exp_avg: float32 [16, 512, 512], P('fsdp', 'dp'), may hold values from -2 to 2
- exp_avg_sq: float32 [16, 512, 512], P('fsdp', 'dp'), may hold values from 0.25 to 4
Outputs:
- basis_new: bfloat16 [16, 2, 512, 512], P('fsdp')
- exp_avg_new: float32 [16, 512, 512], P('fsdp', 'dp')
- exp_avg_sq_new: float32 [16, 512, 512], P('fsdp', 'dp')
- update: bfloat16 [16, 512, 512], P('fsdp', 'dp')
Inputs may be any that keep to these rules, and one draw needn't show every extreme that they name: `partials`: for every block and factor the sum over the 32 replicas is symmetric and positive definite. `owner_table`: distinct data indices, 2 apart in a rotated order, the largest 32 - 1.
All inputs are finite; a program needn't handle non-finite values.
Results may differ from a plain program's by a relative error of at most 0.014.
Values may be sent and summed in bfloat16 or wider, within the bound.
No kernel may reach another device: no remote copies, remote signals or barrier semaphores. Data moves between devices by JAX's collectives and lax.ppermute only.
A program may use at most 64 MiB of HBM per device.

v0:
```python
import jax
import jax.numpy as jnp
from jax import lax
from jax.sharding import PartitionSpec as P

STEPS = 2


FULL = lax.Precision.HIGHEST


def spread(value, axis, source):
    kept = jnp.where(lax.axis_index(axis) == source, value, 0).astype(value.dtype)
    return lax.psum(kept, axis)


def orthonormal_step(factor, initial):
    images = jnp.dot(factor, initial, precision=FULL, preferred_element_type=jnp.float32)
    gram_matrix = jnp.dot(images.T, images, precision=FULL, preferred_element_type=jnp.float32)
    lower_factor = jnp.linalg.cholesky(gram_matrix)
    return lax.linalg.triangular_solve(
        lower_factor, images, left_side=False, lower=True, transpose_a=True
    )


def refresh_bases(factors, initial):
    current = initial.astype(jnp.float32)
    for repeat in range(STEPS):
        current = jax.vmap(orthonormal_step)(factors, current)
    return current.astype(jnp.bfloat16)


def on_device(partials, basis_store, owner_table, grad, exp_avg, exp_avg_sq):
    height = grad.shape[1]
    column = lax.axis_index("fsdp")
    replica = lax.axis_index("dp")
    positions = jnp.arange(owner_table.shape[0], dtype=jnp.int32)
    owner = jnp.sum(jnp.where(positions == column, owner_table, 0))
    factors = lax.psum(partials[0, 0].astype(jnp.float32), "dp")
    stored = basis_store[0, 0]
    computed = lax.cond(
        replica == owner, lambda: refresh_bases(factors, stored), lambda: jnp.zeros_like(stored)
    )
    shipped = spread(jnp.stack([computed, stored]), "dp", owner)
    fresh = shipped[0]
    previous = shipped[1]
    left_new = fresh[0]
    right_new = fresh[1]
    left_old = previous[0]
    right_old = previous[1]
    offset = replica * height
    left_rows = lax.dynamic_slice_in_dim(left_new, offset, height, 0)
    old_columns = lax.dynamic_slice_in_dim(left_old, offset, height, 1)
    projected = jnp.dot(grad[0], right_new, preferred_element_type=jnp.float32).astype(jnp.bfloat16)
    contract_first = (((0,), (0,)), ((), ()))
    contract_second = (((1,), (1,)), ((), ()))
    right_turn = lax.dot_general(
        right_new, right_old, contract_first, preferred_element_type=jnp.float32
    )
    left_turn = lax.dot_general(
        left_new, old_columns, contract_first, preferred_element_type=jnp.float32
    )
    moment_back = lax.dot_general(
        exp_avg[0], right_turn, contract_second, precision=FULL, preferred_element_type=jnp.float32
    )
    left_piece = left_rows
    gradient_term = lax.dot_general(
        left_piece, projected, contract_first, preferred_element_type=jnp.float32
    )
    moment_term = jnp.dot(
        left_turn, moment_back, precision=FULL, preferred_element_type=jnp.float32
    )
    rotated = lax.psum_scatter(
        jnp.stack([gradient_term, moment_term], axis=1), "dp", scatter_dimension=0, tiled=True
    )
    gradient_rot = rotated[:, 0]
    moment_rot = rotated[:, 1]
    moment_new = 0.9 * moment_rot + 0.1 * gradient_rot
    square_new = 0.95 * exp_avg_sq[0] + 0.05 * gradient_rot * gradient_rot
    direction = (moment_new / (jnp.sqrt(square_new) + 1e-08)).astype(jnp.bfloat16)
    returned = lax.dot_general(
        direction, right_new, contract_second, preferred_element_type=jnp.float32
    ).astype(jnp.bfloat16)
    left_piece = left_rows
    update = jnp.dot(
        left_piece,
        lax.all_gather(returned, "dp", axis=0, tiled=True),
        preferred_element_type=jnp.float32,
    )
    return (fresh[None], moment_new[None], square_new[None], update.astype(jnp.bfloat16)[None])


def solution(mesh):
    in_specs = (
        P("dp", "fsdp", None, None, None),
        P("dp", "fsdp", None, None, None),
        P(),
        P("fsdp", "dp", None),
        P("fsdp", "dp", None),
        P("fsdp", "dp", None),
    )
    out_specs = (
        P("fsdp", None, None, None),
        P("fsdp", "dp", None),
        P("fsdp", "dp", None),
        P("fsdp", "dp", None),
    )
    return jax.shard_map(
        on_device, mesh=mesh, in_specs=in_specs, out_specs=out_specs, check_vma=False
    )
```

profile of v0, /device:TPU:1, one launch (start us, length us, event | category | flops | bytes accessed | tf_op | source)
XLA Modules:
  0.0 1416.7 jit_solution(5202837085224911765)
XLA Ops:
  7.2 0.0 copy-start
  7.2 0.0 copy-start.15
  7.2 0.0 copy-start.5
  7.2 0.0 all-reduce.4.cloned.1.call-start
  7.2 2.9 bitcast_convert_fusion
  10.1 0.0 all-reduce.4.cloned.1.call-update
  10.2 0.0 all-reduce.6.cloned.1.call-start
  10.2 0.0 copy-done.15
  10.2 0.6 fusion.107
  11.5 291.6 %all-reduce.4.cloned.1.call-done = f32[2,512,512]{2,1,0:T(8,128)} async-done(((f32[2,512,512]{2,1,0:T(8,128)}), f32[2,512,512]{2,1,0:T(8,128)}) %all-reduce.4.cloned.1.call-update) | async-done | bytes 2097168 | tf_op jit(solution)/shard_map/psum | solution.py:39
  303.1 0.0 copy-done.5
  303.2 1.0 conditional.1
  303.2 1.0 stack.13.clone
  304.2 2.7 maximum_select_fusion
  306.9 0.0 all-reduce.6.cloned.1.call-update
  307.0 0.0 reduce-scatter.2.cloned.1.call-start
  307.0 900.7 %all-reduce.6.cloned.1.call-done = bf16[2,2,512,512]{3,2,1,0:T(8,128)(2,1)} async-done(((bf16[2,2,512,512]{3,2,1,0:T(8,128)(2,1)}), bf16[2,2,512,512]{3,2,1,0:T(8,128)(2,1)}) %all-reduce.6.cloned.1.call-update) | async-done | bytes 2097168 | tf_op jit(solution)/shard_map/psum | solution.py:14
  1207.7 1.8 fusion.81
  1209.5 1.0 fusion.92
  1210.5 0.0 copy-start.14
  1210.5 0.9 fusion.119
  1211.4 0.4 fusion.82
  1211.8 1.0 convolution_bitcast_fusion
  1212.8 2.5 convolution_bitcast_fusion.1
  1215.3 2.7 pad_maximum_fusion
  1218.0 0.0 reduce-scatter.2.cloned.1.call-update
  1218.0 1.0 slice.198
  1219.1 143.3 %reduce-scatter.2.cloned.1.call-done = f32[16,2,512]{2,0,1:T(8,128)} async-done(((f32[512,2,512]{2,0,1:T(8,128)}), f32[16,2,512]{2,0,1:T(8,128)}) %reduce-scatter.2.cloned.1.call-update) | async-done | bytes 65552 | tf_op jit(solution)/shard_map/reduce_scatter | solution.py:73
  1362.3 1.0 convolution_convert_fusion.2
  1363.3 43.9 %all_gather.3 = bf16[512,512]{1,0:T(8,128)(2,1)S(1)} all-gather(bf16[16,512]{1,0:T(8,128)(2,1)S(1)} %convolution_convert_fusion.2), channel_id=1, replica_groups=mesh['dp'=32,'fsdp'=16] {'dp'}, dimensions={0}, use_global_device_ids=true | all-gather | bytes 540672 | tf_op jit(solution)/shard_map/all_gather | solution.py:87
  1407.2 1.5 fusion.80
  1408.8 1.4 fusion.86
  (6 shorter events, 0.0 us)
Async XLA Ops:
  7.2 1202.4 %copy-start = (f32[1,16,512]{2,1,0:T(8,128)S(1)}, f32[1,16,512]{2,1,0:T(8,128)}, u32[]{:S(2)}) copy-start(f32[1,16,512]{2,1,0:T(8,128)} %param.15) | copy-start | bytes 98308
  7.2 3.0 copy-start.15
  7.2 296.0 %copy-start.5 = (bf16[1,1,2,512,512]{4,3,2,1,0:T(8,128)(2,1)S(1)}, bf16[1,1,2,512,512]{4,3,2,1,0:T(8,128)(2,1)}, u32[]{:S(2)}) copy-start(bf16[1,1,2,512,512]{4,3,2,1,0:T(8,128)(2,1)} %param.12) | copy-start | bytes 3145732
  7.2 295.9 %all-reduce.4.cloned.1.call-start = ((), (), s32[]{:S(2)}) async-start(), calls=%async_computation.1 | async-start | bytes 4194304 | tf_op jit(solution)/shard_map/psum | solution.py:39
  10.2 1197.5 %all-reduce.6.cloned.1.call-start = ((), (), s32[]{:S(2)}) async-start(), calls=%async_computation.2 | async-start | bytes 4194304 | tf_op jit(solution)/shard_map/psum | solution.py:14
  307.0 1055.4 %reduce-scatter.2.cloned.1.call-start = ((), (), s32[]{:S(2)}) async-start(), calls=%async_computation.3 | async-start | bytes 2162688 | tf_op jit(solution)/shard_map/reduce_scatter | solution.py:73
  1207.7 2.8 copy-start.4
  1210.5 2.3 copy-start.14
  1218.0 144.3 %copy-start.13 = (f32[1,16,512]{2,1,0:T(8,128)S(1)}, f32[1,16,512]{2,1,0:T(8,128)}, u32[]{:S(2)}) copy-start(f32[1,16,512]{2,1,0:T(8,128)} %param.16) | copy-start | bytes 98308
Sparse Core Ops, SparseCore 0:
  11.0 292.1 all-reduce.3
  307.1 900.5 all-reduce.5
  1218.1 144.1 reduce-scatter.1
where the time goes:
time: 1420 us
  waiting for transfers between devices  1340 us (94%)
  blocking collectives  43.9 us (3%)
  between operations  14.5 us (1%)
    psum x1, waiting for transfers between devices, spread(): return lax.psum(kept, axis)  901 us
    psum x1, waiting for transfers between devices, on_device(): factors = lax.psum(partials[0, 0].astype(jnp.float32), 'dp')  292 us
    reduce_scatter x1, waiting for transfers between devices, on_device(): lax.psum_scatter(jnp.stack([gradient_term, moment_term], axis=1), 'dp', s...  143 us
    all_gather x1, blocking collectives, on_device(): lax.all_gather(returned, 'dp', axis=0, tiled=True)  43.9 us
  transfers between devices with their start and end apart: 3, of which 3 were waited for; matrix products, arithmetic and copies ran while one was open for 0% of the time, Pallas kernels for 0%

commit v1 on v0

v1 whole, which is shorter than its diff:
```python
import functools

import jax
import jax.numpy as jnp
from jax import lax
from jax.experimental import pallas as pl
from jax.experimental.pallas import tpu as pltpu
from jax.sharding import PartitionSpec as P

F32 = jnp.float32
BF16 = jnp.bfloat16
FULL = lax.Precision.HIGHEST
B = 128
N = 512
NB = N // B
CHIPS = 16
UPPER = [(i, j) for i in range(NB) for j in range(i, NB)]
PACK = len(UPPER) * B
PF = PACK // CHIPS
PQ = N * NB // CHIPS
PIECE = PF + PQ
STEP = 16
RELAX = (1.4, 1.4, 1.4, 1.4, 1.0, 1.0)
START = 0.6
TOLERANCE = 0.03
PIVOT = 1e-4

PARAMS = pltpu.CompilerParams(vmem_limit_bytes=48 * 1024 * 1024)
SMEM = pl.BlockSpec(memory_space=pltpu.SMEM)
VMEM = pl.BlockSpec(memory_space=pltpu.VMEM)


def spec(i):
    return slice(i * B, (i + 1) * B)


def dot(a, b):
    return jnp.dot(a, b, preferred_element_type=F32)


def dot_tn(a, b):
    return lax.dot_general(a, b, (((0,), (0,)), ((), ())), preferred_element_type=F32)


def dot_nt(a, b):
    return lax.dot_general(a, b, (((1,), (1,)), ((), ())), preferred_element_type=F32)


def split(x):
    high = x.astype(BF16)
    return high, (x - high.astype(F32)).astype(BF16)


def dot3(a, b, op=dot):
    ah, al = a
    bh, bl = b
    return op(ah, bh) + (op(ah, bl) + op(al, bh))


def pieces(t):
    row, end = t * B, (t + 1) * B
    while row < end:
        piece = row // PF
        count = min(end, (piece + 1) * PF) - row
        yield piece, row - piece * PF, row - t * B, count
        row += count


def pack_kernel(meta, part, out):
    other = 1 - meta[0]
    for t, (i, j) in enumerate(UPPER):
        out[t * B : (t + 1) * B, :] = part[other, spec(i), spec(j)]


def pair_kernel(meta, part, got, got_basis, basis, out):
    core = meta[0]
    for t, (i, j) in enumerate(UPPER):
        total = part[core, spec(i), spec(j)].astype(F32) + got[t * B : (t + 1) * B, :].astype(F32)
        total = total.astype(BF16)
        for piece, at, row, count in pieces(t):
            out[piece, at : at + count, :] = total[row : row + count]

    @pl.when(core == 0)
    def _():
        for k in range(CHIPS):
            out[k, PF:, :] = got_basis[spec(k % NB), spec(k // NB)]

    @pl.when(core == 1)
    def _():
        for k in range(CHIPS):
            out[k, PF:, :] = basis[1, spec(k % NB), spec(k // NB)]


def sum_kernel(meta, got, out):
    owner = meta[2]
    total = got[0, :PF, :].astype(F32)
    for k in range(1, CHIPS):
        total = total + got[k, :PF, :].astype(F32)
    total = total.astype(BF16)
    chosen = got[owner, PF:, :]
    for k in range(CHIPS):
        out[k, :PF, :] = total
        out[k, PF:, :] = chosen


def unpack_basis(got, out):
    for k in range(CHIPS):
        out[spec(k % NB), spec(k // NB)] = got[k, PF:, :]


def grid_of(n):
    return (
        lax.broadcasted_iota(jnp.int32, (n, n), 0),
        lax.broadcasted_iota(jnp.int32, (n, n), 1),
    )


def eliminate(gram, current):
    lane = lax.broadcasted_iota(jnp.int32, (1, N), 1)
    sub = lax.broadcasted_iota(jnp.int32, (N, 1), 0)

    def step(j, carry):
        row = gram[pl.ds(j, 1), :]
        pivot = jnp.sum(jnp.where(lane == j, row, 0.0), axis=1, keepdims=True)
        ratio = jnp.where(lane > j, row / pivot, 0.0)
        g = gram[...]
        column = jnp.sum(jnp.where(lane == j, g, 0.0), axis=1, keepdims=True)
        gram[...] = g - jnp.where(sub > j, column, 0.0) * ratio
        a = current[...]
        column = jnp.sum(jnp.where(lane == j, a, 0.0), axis=1, keepdims=True)
        current[...] = jnp.where(lane == j, a * lax.rsqrt(pivot), a - column * ratio)
        return carry

    lax.fori_loop(0, N, step, 0)


def basis_kernel(got, out, factor, start, packed, gram, images):
    for k in range(CHIPS):
        packed[k * PF : (k + 1) * PF, :] = got[k, :PF, :]
    for t, (i, j) in enumerate(UPPER):
        block = packed[t * B : (t + 1) * B, :]
        factor[spec(i), spec(j)] = block
        if i != j:
            factor[spec(j), spec(i)] = block.T
    unpack_basis(got, start)

    f = factor[...]
    ah, al = split(dot(f, start[...]))
    t = dot(f, ah) + dot(f, al)
    images[...] = t
    th, tl = split(t)
    gram[...] = dot3((th, tl), (th, tl), dot_tn)

    rows, cols = grid_of(B)
    eye = rows == cols
    unit = jnp.where(eye, 1.0, 0.0)
    lengths = jnp.sum(t * t, axis=0, keepdims=True)
    fault = jnp.zeros((B, B), F32)
    for k in range(NB):
        h = gram[spec(k), spec(k)]
        on = jnp.where(eye, h, 0.0)
        pivots = jnp.sum(on, axis=0, keepdims=True)
        fault = jnp.where(pivots > PIVOT * lengths[:, spec(k)], fault, 1.0)
        down = lax.rsqrt(jnp.sum(on, axis=1, keepdims=True)) * START
        across = lax.rsqrt(pivots) * START
        h = h * down * across
        p = None
        for step, relax in enumerate(RELAX):
            e = h - unit
            weights = jnp.where(eye, 0.5 * relax, relax)
            upper = unit - jnp.where(rows <= cols, e * weights, 0.0)
            us = split(upper)
            if step < len(RELAX) - 1:
                lower = unit - jnp.where(rows >= cols, e * weights, 0.0)
                hu = dot3(split(h), us)
                h = dot3(split(lower), split(hu))
            else:
                fault = jnp.where(jnp.abs(e) < TOLERANCE, fault, 1.0)
            p = upper if p is None else dot3(split(p), us)
        s = p * down
        ss = split(s)
        q = dot3(split(images[:, spec(k)]), ss)
        out[:, spec(k)] = q.astype(BF16)
        if k < NB - 1:
            rest = slice((k + 1) * B, N)
            r = dot3(split(s.T), split(gram[spec(k), rest]))
            rs = split(r)
            gram[rest, rest] = gram[rest, rest] - dot3(rs, rs, dot_tn)
            images[:, rest] = images[:, rest] - dot3(split(q), rs)

    @pl.when(jnp.max(fault) > 0.0)
    def _():
        images[...] = start[...].astype(F32)
        for repeat in range(2):
            image = jnp.dot(
                factor[...].astype(F32), images[...], precision=FULL, preferred_element_type=F32
            )
            images[...] = image
            gram[...] = lax.dot_general(
                image, image, (((0,), (0,)), ((), ())), precision=FULL, preferred_element_type=F32
            )
            eliminate(gram, images)
        out[...] = images[...].astype(BF16)


def turn_kernel(meta, mine, theirs, rows, out, bases):
    core = meta[0]
    for k in range(CHIPS):
        bases[core, spec(k % NB), spec(k // NB)] = mine[k, PF:, :]
        bases[1 - core, spec(k % NB), spec(k // NB)] = theirs[k, PF:, :]
    moment = rows[:, STEP : 2 * STEP, :].reshape(N, N)
    half = dot(bases[0], moment).astype(BF16)
    out[...] = dot_nt(half, bases[1]).astype(BF16)


def final_kernel(meta, mine, theirs, turned, rows, square, fresh, moment_out, square_out, update, mom, rot):
    core = meta[0]
    fresh[core] = mine[...]
    fresh[1 - core] = theirs[...]
    left = fresh[0]
    right = fresh[1]
    grad = rows[:, :STEP, :].reshape(N, N)
    projected = dot(grad, right).astype(BF16)
    moment = dot(turned[...], right).astype(BF16)
    gradient_rot = dot_tn(left, projected)
    moment_rot = dot_tn(left, moment)
    new = 0.9 * moment_rot + 0.1 * gradient_rot
    mom[...] = new
    rot[...] = gradient_rot
    squares = rows[:, 2 * STEP :, :].reshape(N, N).astype(F32)
    level = 0.95 * squares + 0.05 * gradient_rot * gradient_rot
    direction = (new / (jnp.sqrt(level) + 1e-08)).astype(BF16)
    returned = dot_nt(direction, right).astype(BF16)
    at = pl.ds(pl.multiple_of(meta[1] * STEP, STEP), STEP)
    moment_out[...] = mom[at, :]
    own = rot[at, :]
    square_out[...] = 0.95 * square[...] + 0.05 * own * own
    update[...] = dot(fresh[0, at, :], returned).astype(BF16)


def shape(dims, dtype):
    return jax.ShapeDtypeStruct(dims, dtype)


def call(kernel, name, out, specs, scratch=(), flops=0):
    return pl.pallas_call(
        kernel,
        name=name,
        out_shape=out,
        in_specs=specs,
        scratch_shapes=list(scratch),
        compiler_params=PARAMS,
        cost_estimate=pl.CostEstimate(flops=flops, bytes_accessed=2**21, transcendentals=0),
    )


def on_device(partials, basis_store, owner_table, grad, exp_avg, exp_avg_sq):
    column = lax.axis_index("fsdp")
    replica = lax.axis_index("dp")
    positions = jnp.arange(owner_table.shape[0], dtype=jnp.int32)
    owner = jnp.sum(jnp.where(positions == column, owner_table, 0))
    core = replica % 2
    meta = jnp.stack([core, replica, owner // 2]).astype(jnp.int32)
    devices = 2 * CHIPS
    swap = [(i, i ^ 1) for i in range(devices)]
    down = [(i, i - 1) for i in range(1, devices, 2)]
    groups = [list(range(c, devices, 2)) for c in range(2)]

    rows = jnp.concatenate([grad[0], exp_avg[0].astype(BF16), exp_avg_sq[0].astype(BF16)], axis=0)
    rows = lax.all_gather(rows, "dp", axis=0, tiled=False)

    part = partials[0, 0]
    stored = basis_store[0, 0]
    got_basis = lax.ppermute(stored[0], "dp", down)
    packed = call(pack_kernel, "pack", shape((PACK, B), BF16), [SMEM, VMEM])(meta, part)
    got = lax.ppermute(packed, "dp", swap)
    payload = call(pair_kernel, "pair", shape((CHIPS, PIECE, B), BF16), [SMEM] + [VMEM] * 4)(
        meta, part, got, got_basis, stored
    )
    got = lax.all_to_all(payload, "dp", 0, 0, tiled=True, axis_index_groups=groups)
    payload = call(sum_kernel, "sum", shape((CHIPS, PIECE, B), BF16), [SMEM, VMEM])(meta, got)
    whole = lax.all_to_all(payload, "dp", 0, 0, tiled=True, axis_index_groups=groups)
    whole_other = lax.ppermute(whole, "dp", swap)
    mine = call(
        basis_kernel,
        "basis",
        shape((N, N), BF16),
        [VMEM],
        [
            pltpu.VMEM((N, N), BF16),
            pltpu.VMEM((N, N), BF16),
            pltpu.VMEM((PACK, B), BF16),
            pltpu.VMEM((N, N), F32),
            pltpu.VMEM((N, N), F32),
        ],
        flops=2**34,
    )(whole)
    theirs = lax.ppermute(mine, "dp", swap)
    turned = call(
        turn_kernel, "turn", shape((N, N), BF16), [SMEM] + [VMEM] * 3, [pltpu.VMEM((2, N, N), BF16)], flops=2**30
    )(meta, whole, whole_other, rows)
    fresh, moment_new, square_new, update = call(
        final_kernel,
        "final",
        (
            shape((2, N, N), BF16),
            shape((STEP, N), F32),
            shape((STEP, N), F32),
            shape((STEP, N), BF16),
        ),
        [SMEM] + [VMEM] * 5,
        [pltpu.VMEM((N, N), F32), pltpu.VMEM((N, N), F32)],
        flops=2**32,
    )(meta, mine, theirs, turned, rows, exp_avg_sq[0])
    return fresh[None], moment_new[None], square_new[None], update[None]


def solution(mesh):
    in_specs = (
        P("dp", "fsdp", None, None, None),
        P("dp", "fsdp", None, None, None),
        P(),
        P("fsdp", "dp", None),
        P("fsdp", "dp", None),
        P("fsdp", "dp", None),
    )
    out_specs = (
        P("fsdp", None, None, None),
        P("fsdp", "dp", None),
        P("fsdp", "dp", None),
        P("fsdp", "dp", None),
    )
    return jax.shard_map(
        on_device, mesh=mesh, in_specs=in_specs, out_specs=out_specs, check_vma=False
    )
```

time: 1420 us -> 512 us (0.36)
  waiting for transfers between devices: 1340 us -> 19.7 us
  Pallas kernels: 0 us -> 423 us
  starting transfers between devices: 0.12 us -> 22.7 us
  blocking collectives: 43.9 us -> 24.5 us
    psum x2 -> x0, waiting for transfers between devices: 1190 us -> none  [the longest x1 901 us: spread(): return lax.psum(kept, axis)]
    pallas_call x0 -> x6, Pallas kernels: none -> 423 us  [the longest x1 414 us: on_device(): call(basis_kernel, 'basis', shape((N, N), BF16), [VMEM], [pltpu.VMEM((N,...]
    reduce_scatter x1 -> x0, waiting for transfers between devices: 143 us -> none  [on_device(): lax.psum_scatter(jnp.stack([gradient_term, moment_term], axis=1), 'dp', s...]
    all_gather x1 -> x0, blocking collectives: 43.9 us -> none  [on_device(): lax.all_gather(returned, 'dp', axis=0, tiled=True)]
    all_to_all x0 -> x1, blocking collectives: none -> 24.5 us  [on_device(): lax.all_to_all(payload, 'dp', 0, 0, tiled=True, axis_index_groups=groups)]
    all_to_all x0 -> x1, waiting for transfers between devices: none -> 18.1 us  [on_device(): lax.all_to_all(payload, 'dp', 0, 0, tiled=True, axis_index_groups=groups)]
    ppermute x0 -> x4, starting transfers between devices: none -> 17.9 us  [the longest x1 8.82 us: on_device(): got_basis = lax.ppermute(stored[0], 'dp', down)]
  transfers between devices with their start and end apart: 3 -> 6, of which waited for: 3 -> 2; matrix products, arithmetic and copies ran while one was open for 0% -> 0% of each run, Pallas kernels for 0% -> 82%
where the time goes in v1:
time: 512 us; the launch traced here: 511 us
  Pallas kernels  423 us (83%)
  blocking collectives  24.5 us (5%)
  starting transfers between devices  22.7 us (4%)
  waiting for transfers between devices  19.7 us (4%)
  between operations  16.8 us (3%)
    pallas_call x1, Pallas kernels, on_device(): call(basis_kernel, 'basis', shape((N, N), BF16), [VMEM], [pltpu.VMEM((N,...  414 us
    all_to_all x1, blocking collectives, on_device(): lax.all_to_all(payload, 'dp', 0, 0, tiled=True, axis_index_groups=groups)  24.5 us
    all_to_all x1, waiting for transfers between devices, on_device(): lax.all_to_all(payload, 'dp', 0, 0, tiled=True, axis_index_groups=groups)  18.1 us
  transfers between devices with their start and end apart: 6, of which 2 were waited for; matrix products, arithmetic and copies ran while one was open for 0% of the time, Pallas kernels for 82%

profile of v1, /device:TPU:1, one launch (start us, length us, event | category | flops | bytes accessed | tf_op | source)
XLA Modules:
  0.0 511.0 jit_solution(16031074177446020884)
XLA Ops:
  7.2 0.0 copy-start
  7.2 0.0 copy-start.1
  7.2 1.2 slice_bitcast_fusion
  8.4 8.8 %collective-permute-start.1 = (bf16[512,512]{1,0:T(8,128)(2,1)S(1)}, bf16[512,512]{1,0:T(8,128)(2,1)S(1)}, u32[]{:S(2)}, u32[]{:S(2)}) collective-permute-start(bf16[512,512]{1,0:T(8,128)(2,1)S(1)} %slice_bitcast_fusion), channel_id=1, source_target_pairs={{16,0},{48,32},{80,64},{112,96},{144,128},{176,160},{208,192},{240... | collective-permute-start | bytes 1572872 | tf_op jit(solution)/shard_map/ppermute | solution.py:274
  17.2 1.3 fusion
  21.2 0.1 pad_add_fusion.meta
  21.2 0.0 copy-done
  21.2 0.6 pack.1
  21.8 1.9 collective-permute-start
  23.8 1.6 collective-permute-done.got
  25.4 0.0 collective-permute-done.1.got_basis
  25.4 0.0 copy-done.1
  25.4 0.7 pair.1
  26.1 24.5 %all_to_all.10.got = bf16[16,208,128]{2,1,0:T(8,128)(2,1)S(1)} all-to-all(bf16[16,208,128]{2,1,0:T(8,128)(2,1)S(1)} %pair.1), channel_id=1, replica_groups={{0,32,64,96,128,160,192,224,256,288,320,352,384,416,448,480},{16,48,80,..., dimensions={0} | all-to-all | bytes 1703936 | tf_op jit(solution)/shard_map/all_to_all | solution.py:280
  50.6 1.5 sum.1
  52.2 4.8 all-to-all-start.1
  57.0 0.0 all-gather.3.cloned.1.call-start
  57.0 0.0 copy-done.2
  57.0 0.0 copy-done.5
  57.0 0.0 copy-done.6
  57.0 0.6 pad_maximum_fusion
  57.7 0.0 all-gather.3.cloned.1.call-update
  57.7 18.1 %all-to-all-done.1.got.mine = bf16[16,208,128]{2,1,0:T(8,128)(2,1)S(1)} async-done(((bf16[16,208,128]{2,1,0:T(8,128)(2,1)}), bf16[16,208,128]{2,1,0:T(8,128)(2,1)S(1)}, u32[]{:S(2)}, u32[]{:S(2)}) %all-to-all-start.1) | async-done | bytes 852000 | tf_op jit(solution)/shard_map/all_to_all | solution.py:282
  75.8 5.2 %collective-permute-start.3 = (bf16[16,208,128]{2,1,0:T(8,128)(2,1)S(1)}, bf16[16,208,128]{2,1,0:T(8,128)(2,1)S(1)}, u32[]{:S(2)}, u32[]{:S(2)}) collective-permute-start(bf16[16,208,128]{2,1,0:T(8,128)(2,1)S(1)} %all-to-all-done.1.got.mine), channel_id=1, source_target_pairs={{0,16},{16,0},{32,48},{48,32},{64,80},{80,64},{96,112},{112,96},{1... | collective-permute-start | bytes 2555912 | tf_op jit(solution)/shard_map/ppermute | solution.py:283
  81.0 414.5 %basis.1.mine = bf16[512,512]{1,0:T(8,128)(2,1)} custom-call(bf16[16,208,128]{2,1,0:T(8,128)(2,1)S(1)} %all-to-all-done.1.got.mine), custom_call_target="tpu_custom_call" | custom-call | flops 17179869184 | bytes 2097152 | tf_op jit(solution)/shard_map/basis/pallas_call | solution.py:284
  495.5 1.9 collective-permute-start.2
  497.4 0.0 all-gather.3.cloned.1.call-done
  497.5 0.0 collective-permute-done.3.theirs
  497.5 1.4 copy-done.3
  498.9 1.4 turn.1.turned
  500.3 0.0 collective-permute-done.2.theirs
  500.3 3.9 final.1
  (7 shorter events, 0.0 us)
Async XLA Ops:
  7.2 14.1 %copy-start = (bf16[1,1,2,512,512]{4,3,2,1,0:T(8,128)(2,1)S(1)}, bf16[1,1,2,512,512]{4,3,2,1,0:T(8,128)(2,1)}, u32[]{:S(2)}) copy-start(bf16[1,1,2,512,512]{4,3,2,1,0:T(8,128)(2,1)} %param.6) | copy-start | bytes 3145732
  7.2 18.2 %copy-start.1 = (bf16[1,1,2,512,512]{4,3,2,1,0:T(8,128)(2,1)S(1)}, bf16[1,1,2,512,512]{4,3,2,1,0:T(8,128)(2,1)}, u32[]{:S(2)}) copy-start(bf16[1,1,2,512,512]{4,3,2,1,0:T(8,128)(2,1)} %param.7) | copy-start | bytes 3145732
  8.4 17.0 %collective-permute-start.1 = (bf16[512,512]{1,0:T(8,128)(2,1)S(1)}, bf16[512,512]{1,0:T(8,128)(2,1)S(1)}, u32[]{:S(2)}, u32[]{:S(2)}) collective-permute-start(bf16[512,512]{1,0:T(8,128)(2,1)S(1)} %slice_bitcast_fusion), channel_id=1, source_target_pairs={{16,0},{48,32},{80,64},{112,96},{144,128},{176,160},{208,192},{240... | collective-permute-start | bytes 1572872 | tf_op jit(solution)/shard_map/ppermute | solution.py:274
  21.8 3.5 collective-permute-start
  50.6 6.4 %copy-start.2 = (f32[1,16,512]{2,1,0:T(8,128)S(1)}, f32[1,16,512]{2,1,0:T(8,128)}, u32[]{:S(2)}) copy-start(f32[1,16,512]{2,1,0:T(8,128)} %param.11) | copy-start | bytes 98308
  50.6 6.4 %copy-start.5 = (f32[1,16,512]{2,1,0:T(8,128)S(1)}, f32[1,16,512]{2,1,0:T(8,128)}, u32[]{:S(2)}) copy-start(f32[1,16,512]{2,1,0:T(8,128)} %param.10) | copy-start | bytes 98308
  50.6 6.4 %copy-start.6 = (bf16[1,16,512]{2,1,0:T(8,128)(2,1)S(1)}, bf16[1,16,512]{2,1,0:T(8,128)(2,1)}, u32[]{:S(2)}) copy-start(bf16[1,16,512]{2,1,0:T(8,128)(2,1)} %param.9) | copy-start | bytes 49156
  52.2 23.6 %all-to-all-start.1 = ((bf16[16,208,128]{2,1,0:T(8,128)(2,1)}), bf16[16,208,128]{2,1,0:T(8,128)(2,1)S(1)}, u32[]{:S(2)}, u32[]{:S(2)}) async-start(bf16[16,208,128]{2,1,0:T(8,128)(2,1)} %sum.1), calls=%async_computation.1 | async-start | bytes 1703936 | tf_op jit(solution)/shard_map/all_to_all | solution.py:282
  57.0 440.5 %all-gather.3.cloned.1.call-start = ((), (), s32[]{:S(2)}) async-start(), calls=%async_computation.2 | async-start | bytes 1622016 | tf_op jit(solution)/shard_map/all_gather | solution.py:270
  75.8 421.7 %collective-permute-start.3 = (bf16[16,208,128]{2,1,0:T(8,128)(2,1)S(1)}, bf16[16,208,128]{2,1,0:T(8,128)(2,1)S(1)}, u32[]{:S(2)}, u32[]{:S(2)}) collective-permute-start(bf16[16,208,128]{2,1,0:T(8,128)(2,1)S(1)} %all-to-all-done.1.got.mine), channel_id=1, source_target_pairs={{0,16},{16,0},{32,48},{48,32},{64,80},{80,64},{96,112},{112,96},{1... | collective-permute-start | bytes 2555912 | tf_op jit(solution)/shard_map/ppermute | solution.py:283
  495.5 4.8 collective-permute-start.2
  497.5 1.4 copy-start.3
  498.9 1.4 copy-start.4
Sparse Core Ops, SparseCore 0:
  59.9 64.9 all-gather.2

commit v2 on v1

--- a/solution.py
+++ b/solution.py
@@ -66,14 +66,19 @@
         row += count
 
 
-def pack_kernel(meta, part, out):
-    other = 1 - meta[0]
+def here():
+    replica = lax.axis_index("dp")
+    return replica, lax.rem(replica, 2)
+
+
+def pack_kernel(part, out):
+    other = 1 - here()[1]
     for t, (i, j) in enumerate(UPPER):
         out[t * B : (t + 1) * B, :] = part[other, spec(i), spec(j)]
 
 
-def pair_kernel(meta, part, got, got_basis, basis, out):
-    core = meta[0]
+def pair_kernel(part, got, got_basis, basis, out):
+    core = here()[1]
     for t, (i, j) in enumerate(UPPER):
         total = part[core, spec(i), spec(j)].astype(F32) + got[t * B : (t + 1) * B, :].astype(F32)
         total = total.astype(BF16)
@@ -83,7 +88,7 @@
     @pl.when(core == 0)
     def _():
         for k in range(CHIPS):
-            out[k, PF:, :] = got_basis[spec(k % NB), spec(k // NB)]
+            out[k, PF:, :] = got_basis[0, spec(k % NB), spec(k // NB)]
 
     @pl.when(core == 1)
     def _():
@@ -91,8 +96,8 @@
             out[k, PF:, :] = basis[1, spec(k % NB), spec(k // NB)]
 
 
-def sum_kernel(meta, got, out):
-    owner = meta[2]
+def sum_kernel(table, got, out):
+    owner = lax.div(table[lax.axis_index("fsdp")], 2)
     total = got[0, :PF, :].astype(F32)
     for k in range(1, CHIPS):
         total = total + got[k, :PF, :].astype(F32)
@@ -203,8 +208,8 @@
         out[...] = images[...].astype(BF16)
 
 
-def turn_kernel(meta, mine, theirs, rows, out, bases):
-    core = meta[0]
+def turn_kernel(mine, theirs, rows, out, bases):
+    core = here()[1]
     for k in range(CHIPS):
         bases[core, spec(k % NB), spec(k // NB)] = mine[k, PF:, :]
         bases[1 - core, spec(k % NB), spec(k // NB)] = theirs[k, PF:, :]
@@ -213,8 +218,8 @@
     out[...] = dot_nt(half, bases[1]).astype(BF16)
 
 
-def final_kernel(meta, mine, theirs, turned, rows, square, fresh, moment_out, square_out, update, mom, rot):
-    core = meta[0]
+def final_kernel(mine, theirs, turned, rows, square, fresh, moment_out, square_out, update, mom, rot):
+    replica, core = here()
     fresh[core] = mine[...]
     fresh[1 - core] = theirs[...]
     left = fresh[0]
@@ -231,7 +236,7 @@
     level = 0.95 * squares + 0.05 * gradient_rot * gradient_rot
     direction = (new / (jnp.sqrt(level) + 1e-08)).astype(BF16)
     returned = dot_nt(direction, right).astype(BF16)
-    at = pl.ds(pl.multiple_of(meta[1] * STEP, STEP), STEP)
+    at = pl.ds(pl.multiple_of(replica * STEP, STEP), STEP)
     moment_out[...] = mom[at, :]
     own = rot[at, :]
     square_out[...] = 0.95 * square[...] + 0.05 * own * own
@@ -255,12 +260,6 @@
 
 
 def on_device(partials, basis_store, owner_table, grad, exp_avg, exp_avg_sq):
-    column = lax.axis_index("fsdp")
-    replica = lax.axis_index("dp")
-    positions = jnp.arange(owner_table.shape[0], dtype=jnp.int32)
-    owner = jnp.sum(jnp.where(positions == column, owner_table, 0))
-    core = replica % 2
-    meta = jnp.stack([core, replica, owner // 2]).astype(jnp.int32)
     devices = 2 * CHIPS
     swap = [(i, i ^ 1) for i in range(devices)]
     down = [(i, i - 1) for i in range(1, devices, 2)]
@@ -271,14 +270,14 @@
 
     part = partials[0, 0]
     stored = basis_store[0, 0]
-    got_basis = lax.ppermute(stored[0], "dp", down)
-    packed = call(pack_kernel, "pack", shape((PACK, B), BF16), [SMEM, VMEM])(meta, part)
+    got_basis = lax.ppermute(stored, "dp", down)
+    packed = call(pack_kernel, "pack", shape((PACK, B), BF16), [VMEM])(part)
     got = lax.ppermute(packed, "dp", swap)
-    payload = call(pair_kernel, "pair", shape((CHIPS, PIECE, B), BF16), [SMEM] + [VMEM] * 4)(
-        meta, part, got, got_basis, stored
+    payload = call(pair_kernel, "pair", shape((CHIPS, PIECE, B), BF16), [VMEM] * 4)(
+        part, got, got_basis, stored
     )
     got = lax.all_to_all(payload, "dp", 0, 0, tiled=True, axis_index_groups=groups)
-    payload = call(sum_kernel, "sum", shape((CHIPS, PIECE, B), BF16), [SMEM, VMEM])(meta, got)
+    payload = call(sum_kernel, "sum", shape((CHIPS, PIECE, B), BF16), [SMEM, VMEM])(owner_table, got)
     whole = lax.all_to_all(payload, "dp", 0, 0, tiled=True, axis_index_groups=groups)
     whole_other = lax.ppermute(whole, "dp", swap)
     mine = call(
@@ -293,12 +292,12 @@
             pltpu.VMEM((N, N), F32),
             pltpu.VMEM((N, N), F32),
         ],
-        flops=2**34,
+        flops=0,
     )(whole)
     theirs = lax.ppermute(mine, "dp", swap)
     turned = call(
-        turn_kernel, "turn", shape((N, N), BF16), [SMEM] + [VMEM] * 3, [pltpu.VMEM((2, N, N), BF16)], flops=2**30
-    )(meta, whole, whole_other, rows)
+        turn_kernel, "turn", shape((N, N), BF16), [VMEM] * 3, [pltpu.VMEM((2, N, N), BF16)], flops=0
+    )(whole, whole_other, rows)
     fresh, moment_new, square_new, update = call(
         final_kernel,
         "final",
@@ -308,10 +307,10 @@
             shape((STEP, N), F32),
             shape((STEP, N), BF16),
         ),
-        [SMEM] + [VMEM] * 5,
+        [VMEM] * 5,
         [pltpu.VMEM((N, N), F32), pltpu.VMEM((N, N), F32)],
-        flops=2**32,
-    )(meta, mine, theirs, turned, rows, exp_avg_sq[0])
+        flops=0,
+    )(mine, theirs, turned, rows, exp_avg_sq[0])
     return fresh[None], moment_new[None], square_new[None], update[None]
 
 

time: 512 us -> 505 us (0.986)
  the two profiles are of different devices: /device:TPU:1 before, /device:TPU:313 now
where the time goes in v2:
time: 505 us; the launch traced here: 504 us
  Pallas kernels  419 us (83%)
  blocking collectives  29.4 us (6%)
  waiting for transfers between devices  19.8 us (4%)
  starting transfers between devices  17.7 us (4%)
  between operations  14.2 us (3%)
    pallas_call x1, Pallas kernels, on_device(): call(basis_kernel, 'basis', shape((N, N), BF16), [VMEM], [pltpu.VMEM((N,...  414 us
    all_to_all x1, blocking collectives, on_device(): lax.all_to_all(payload, 'dp', 0, 0, tiled=True, axis_index_groups=groups)  29.4 us
    all_to_all x1, waiting for transfers between devices, on_device(): lax.all_to_all(payload, 'dp', 0, 0, tiled=True, axis_index_groups=groups)  18.1 us
  transfers between devices with their start and end apart: 6, of which 2 were waited for; matrix products, arithmetic and copies ran while one was open for 0% of the time, Pallas kernels for 82%

profile of v2, /device:TPU:313, one launch (start us, length us, event | category | flops | bytes accessed | tf_op | source)
XLA Modules:
  0.0 504.0 jit_solution(13314871345296954676)
XLA Ops:
  7.2 2.6 collective-permute-start.1
  9.8 0.0 copy-start.2
  9.8 1.2 copy-done.2
  11.0 0.0 copy-start.3
  11.0 0.1 pack.1
  11.1 2.1 collective-permute-start
  13.2 1.6 collective-permute-done.got
  14.8 0.0 collective-permute-done.1.got_basis
  14.8 0.0 copy-done.3
  14.8 1.1 pair.1
  15.9 7.2 %all-to-all-start = ((bf16[16,208,128]{2,1,0:T(8,128)(2,1)}), bf16[16,208,128]{2,1,0:T(8,128)(2,1)S(1)}, u32[]{:S(2)}, u32[]{:S(2)}) async-start(bf16[16,208,128]{2,1,0:T(8,128)(2,1)} %pair.1), calls=%async_computation | async-start | bytes 1703936 | tf_op jit(solution)/shard_map/all_to_all | solution.py:279
  23.0 0.0 all-gather.3.cloned.1.call-start
  23.1 0.0 copy-done.4
  23.1 0.0 copy-done.6
  23.1 0.0 copy-done.7
  23.1 0.6 pad_maximum_fusion
  23.7 0.0 all-gather.3.cloned.1.call-update
  23.8 18.1 %all-to-all-done.got = bf16[16,208,128]{2,1,0:T(8,128)(2,1)S(1)} async-done(((bf16[16,208,128]{2,1,0:T(8,128)(2,1)}), bf16[16,208,128]{2,1,0:T(8,128)(2,1)S(1)}, u32[]{:S(2)}, u32[]{:S(2)}) %all-to-all-start) | async-done | bytes 852000 | tf_op jit(solution)/shard_map/all_to_all | solution.py:279
  41.9 0.0 copy-done.5
  41.9 0.7 sum.1
  42.5 29.4 %all_to_all.10.got.mine = bf16[16,208,128]{2,1,0:T(8,128)(2,1)S(1)} all-to-all(bf16[16,208,128]{2,1,0:T(8,128)(2,1)S(1)} %sum.1), channel_id=1, replica_groups={{0,32,64,96,128,160,192,224,256,288,320,352,384,416,448,480},{16,48,80,..., dimensions={0} | all-to-all | bytes 1703936 | tf_op jit(solution)/shard_map/all_to_all | solution.py:281
  71.9 3.9 collective-permute-start.3
  75.9 413.7 %basis.1.mine = bf16[512,512]{1,0:T(8,128)(2,1)S(1)} custom-call(bf16[16,208,128]{2,1,0:T(8,128)(2,1)S(1)} %all_to_all.10.got.mine), custom_call_target="tpu_custom_call" | custom-call | bytes 2097152 | tf_op jit(solution)/shard_map/basis/pallas_call | solution.py:283
  489.6 1.9 collective-permute-start.2
  491.5 0.0 all-gather.3.cloned.1.call-done
  491.5 0.0 collective-permute-done.3.theirs
  491.5 0.0 copy-start
  491.5 1.4 copy-done
  492.9 0.9 turn.1.turned
  493.8 0.0 collective-permute-done.2.theirs
  493.8 0.5 copy-done.1
  494.3 2.8 final.1
  (6 shorter events, 0.0 us)
Async XLA Ops:
  7.2 7.6 %collective-permute-start.1 = (bf16[2,512,512]{2,1,0:T(8,128)(2,1)}, bf16[2,512,512]{2,1,0:T(8,128)(2,1)S(1)}, u32[]{:S(2)}, u32[]{:S(2)}) collective-permute-start(bf16[2,512,512]{2,1,0:T(8,128)(2,1)} %bitcast.16), channel_id=1, source_target_pairs={{16,0},{48,32},{80,64},{112,96},{144,128},{176,160},{208,192},{240... | collective-permute-start | bytes 3145736 | tf_op jit(solution)/shard_map/ppermute | solution.py:273
  9.8 1.2 copy-start.2
  11.0 3.7 copy-start.3
  11.1 3.7 collective-permute-start
  15.8 7.2 %copy-start.4 = (f32[1,16,512]{2,1,0:T(8,128)S(1)}, f32[1,16,512]{2,1,0:T(8,128)}, u32[]{:S(2)}) copy-start(f32[1,16,512]{2,1,0:T(8,128)} %param.11) | copy-start | bytes 98308
  15.9 7.2 %copy-start.6 = (f32[1,16,512]{2,1,0:T(8,128)S(1)}, f32[1,16,512]{2,1,0:T(8,128)}, u32[]{:S(2)}) copy-start(f32[1,16,512]{2,1,0:T(8,128)} %param.10) | copy-start | bytes 98308
  15.9 7.2 %copy-start.7 = (bf16[1,16,512]{2,1,0:T(8,128)(2,1)S(1)}, bf16[1,16,512]{2,1,0:T(8,128)(2,1)}, u32[]{:S(2)}) copy-start(bf16[1,16,512]{2,1,0:T(8,128)(2,1)} %param.9) | copy-start | bytes 49156
  15.9 26.0 %copy-start.5 = (s32[16]{0:T(128)S(1)}, s32[16]{0:T(128)}, u32[]{:S(2)}) copy-start(s32[16]{0:T(128)} %table.1) | copy-start | bytes 196
  15.9 26.0 %all-to-all-start = ((bf16[16,208,128]{2,1,0:T(8,128)(2,1)}), bf16[16,208,128]{2,1,0:T(8,128)(2,1)S(1)}, u32[]{:S(2)}, u32[]{:S(2)}) async-start(bf16[16,208,128]{2,1,0:T(8,128)(2,1)} %pair.1), calls=%async_computation | async-start | bytes 1703936 | tf_op jit(solution)/shard_map/all_to_all | solution.py:279
  23.0 468.5 %all-gather.3.cloned.1.call-start = ((), (), s32[]{:S(2)}) async-start(), calls=%async_computation.2 | async-start | bytes 1622016 | tf_op jit(solution)/shard_map/all_gather | solution.py:269
  71.9 419.6 %collective-permute-start.3 = (bf16[16,208,128]{2,1,0:T(8,128)(2,1)S(1)}, bf16[16,208,128]{2,1,0:T(8,128)(2,1)S(1)}, u32[]{:S(2)}, u32[]{:S(2)}) collective-permute-start(bf16[16,208,128]{2,1,0:T(8,128)(2,1)S(1)} %all_to_all.10.got.mine), channel_id=1, source_target_pairs={{0,16},{16,0},{32,48},{48,32},{64,80},{80,64},{96,112},{112,96},{1... | collective-permute-start | bytes 2555912 | tf_op jit(solution)/shard_map/ppermute | solution.py:282
  489.6 4.3 collective-permute-start.2
  491.5 1.4 copy-start
  492.9 1.4 copy-start.1
Sparse Core Ops, SparseCore 0:
  26.0 66.0 all-gather.2
